TPU v7x, 256 devices: a whole 4x4x8 slice. The times are simulated.
256 devices in a mesh: row: 16 (over y, x_hi, core), col: 16 (over z, x_lo).
Axes of the slice: x: 4 (x_hi: 2, x_lo: 2; x = x_hi * 2 + x_lo), y: 4, z: 8, core: 2. Of those that a mesh axis runs over, the one named last changes fastest.
Arguments:
- observed: float32 [8192, 16384], P('row', 'col'), may hold values from -6 to 6
- mask: int32 [8192, 16384], P('row', 'col'), may hold values 0 or 1
- dual: float32 [8192, 16384], P('row', 'col'), may hold values from -0.1 to 0.9
- row_factor: float32 [8192, 128], P(('row', 'col')), may hold values from -1.75 to 1.75
- col_factor: float32 [16384, 128], P(('col', 'row')), may hold values from -1.75 to 1.75
Outputs:
- row_out: float32 [8192, 128], P(('row', 'col'))
- col_out: float32 [16384, 128], P(('col', 'row'))
- dual_out: float32 [8192, 16384], P('row', 'col')
All inputs are finite; a program needn't handle non-finite values. No bound on the sum of `mask` on one device may be relied on, other than what follows from the above.
Results may differ from a plain program's by a relative error of at most 0.0001.
Values sent between devices are 32-bit elements; how exact they have to be, the bound alone decides.
A program may use at most 64 MiB of HBM per device.

v0:
```python
import jax
import jax.numpy as jnp
from jax import lax
from jax.sharding import PartitionSpec as P

ITERS = 4


tau_level = 0.9
rho_penalty = 1.0
lam_reg = 0.1
eta_step = 0.05
eps_norm = 1e-06


def tile_step(observed, mask, maskf, state, upper, lower):
    pred = jnp.dot(
        upper, lower.T, precision=lax.Precision.HIGHEST, preferred_element_type=jnp.float32
    )
    wide = observed - pred + state / rho_penalty
    clipped = maskf * jnp.clip(wide, -(1.0 - tau_level) / rho_penalty, tau_level / rho_penalty)
    row_term = -rho_penalty * jnp.dot(
        clipped, lower, precision=lax.Precision.HIGHEST, preferred_element_type=jnp.float32
    )
    col_term = -rho_penalty * lax.dot_general(
        clipped,
        upper,
        (((0,), (0,)), ((), ())),
        precision=lax.Precision.HIGHEST,
        preferred_element_type=jnp.float32,
    )
    new_state = jnp.where(mask == 1, rho_penalty * clipped, state)
    return (row_term, col_term, new_state)


def norm_scale(local, count):
    total = lax.psum(local, ("row", "col"))
    return jnp.sqrt(total / count + eps_norm)


def shards(observed, mask, dual, row_factor, col_factor):
    maskf = mask.astype(jnp.float32)
    n_row = lax.axis_size("row")
    n_col = lax.axis_size("col")
    count = (observed.shape[0] * n_row + observed.shape[1] * n_col) * row_factor.shape[1]
    state = dual
    upper = row_factor
    lower = col_factor
    for sweep in range(ITERS):
        upper_blk = lax.all_gather(upper, "col", axis=0, tiled=True)
        lower_blk = lax.all_gather(lower, "row", axis=0, tiled=True)
        row_term, col_term, state = tile_step(observed, mask, maskf, state, upper_blk, lower_blk)
        grad_u = (
            lax.psum_scatter(row_term, "col", scatter_dimension=0, tiled=True) + lam_reg * upper
        )
        grad_v = (
            lax.psum_scatter(col_term, "row", scatter_dimension=0, tiled=True) + lam_reg * lower
        )
        scale = norm_scale(jnp.sum(grad_u * grad_u) + jnp.sum(grad_v * grad_v), count)
        upper = upper - eta_step * grad_u / scale
        lower = lower - eta_step * grad_v / scale
    return (upper, lower, state)


def solution(mesh):
    in_specs = (
        P("row", "col"),
        P("row", "col"),
        P("row", "col"),
        P(("row", "col"), None),
        P(("col", "row"), None),
    )
    out_specs = (P(("row", "col"), None), P(("col", "row"), None), P("row", "col"))
    return jax.shard_map(shards, mesh=mesh, in_specs=in_specs, out_specs=out_specs, check_vma=False)
```

profile of v0, /device:TPU:1, one launch (start us, length us, event | category | flops | bytes accessed | tf_op | source)
XLA Modules:
  0.0 1172.4 jit_solution(11831106333809784852)
XLA Ops:
  7.2 31.9 %all_gather.24 = f32[512,128]{1,0:T(8,128)S(1)} all-gather(f32[32,128]{1,0:T(8,128)} %param.8), channel_id=1, replica_groups=mesh['row'=16,'col'=16] {'col'}, dimensions={0}, use_global_device_ids=true | all-gather | bytes 278528 | tf_op jit(solution)/shard_map/all_gather | solution.py:50
  39.1 34.1 %all_gather.25 = f32[1024,128]{1,0:T(8,128)S(1)} all-gather(f32[64,128]{1,0:T(8,128)} %param.9), channel_id=1, replica_groups=mesh['row'=16,'col'=16] {'row'}, dimensions={0}, use_global_device_ids=true | all-gather | bytes 557056 | tf_op jit(solution)/shard_map/all_gather | solution.py:51
  73.2 5.0 clamp_multiply_fusion.3
  78.2 2.5 convolution_multiply_fusion.7
  80.8 4.2 convolution_multiply_fusion.3
  85.1 45.6 %reduce-scatter.9.cloned.1.call-done = f32[32,128]{1,0:T(8,128)} async-done(((f32[512,128]{1,0:T(8,128)}), f32[32,128]{1,0:T(8,128)}) %reduce-scatter.9.cloned.1.call-update) | async-done | bytes 16400 | tf_op jit(solution)/shard_map/reduce_scatter | solution.py:54
  130.7 1.3 multiply_reduce_fusion.7
  132.1 85.3 %reduce-scatter.11.cloned.1.call-done = f32[64,128]{1,0:T(8,128)} async-done(((f32[1024,128]{1,0:T(8,128)}), f32[64,128]{1,0:T(8,128)}) %reduce-scatter.11.cloned.1.call-update) | async-done | bytes 32784 | tf_op jit(solution)/shard_map/reduce_scatter | solution.py:57
  217.4 1.4 multiply_reduce_fusion.3
  220.0 77.3 %psum.28 = f32[]{:T(128)} all-reduce(f32[]{:T(128)S(6)} %add.87), channel_id=1, replica_groups=mesh['row'=16,'col'=16] {'row','col'}, use_global_device_ids=true, to_apply=%region_4.5 | all-reduce | flops 1 | bytes 8 | tf_op jit(solution)/shard_map/psum | solution.py:37
  298.8 25.3 %all_gather.26 = f32[512,128]{1,0:T(8,128)S(1)} all-gather(f32[32,128]{1,0:T(8,128)S(1)} %divide_subtract_fusion.7), channel_id=1, replica_groups=mesh['row'=16,'col'=16] {'col'}, dimensions={0}, use_global_device_ids=true | all-gather | bytes 278528 | tf_op jit(solution)/shard_map/all_gather | solution.py:50
  324.1 0.8 divide_subtract_fusion.3
  324.9 32.0 %all_gather.27 = f32[1024,128]{1,0:T(8,128)S(1)} all-gather(f32[64,128]{1,0:T(8,128)S(1)} %divide_subtract_fusion.3), channel_id=1, replica_groups=mesh['row'=16,'col'=16] {'row'}, dimensions={0}, use_global_device_ids=true | all-gather | bytes 557056 | tf_op jit(solution)/shard_map/all_gather | solution.py:51
  356.9 5.8 clamp_multiply_fusion.2
  362.7 1.3 copy-done
  364.0 2.5 convolution_multiply_fusion.6
  366.6 5.8 convolution_multiply_fusion.2
  372.5 46.1 %reduce-scatter.13.cloned.1.call-done = f32[32,128]{1,0:T(8,128)} async-done(((f32[512,128]{1,0:T(8,128)}), f32[32,128]{1,0:T(8,128)}) %reduce-scatter.13.cloned.1.call-update) | async-done | bytes 16400 | tf_op jit(solution)/shard_map/reduce_scatter | solution.py:54
  418.6 1.3 multiply_reduce_fusion.6
  419.9 84.6 %reduce-scatter.15.cloned.1.call-done = f32[64,128]{1,0:T(8,128)} async-done(((f32[1024,128]{1,0:T(8,128)}), f32[64,128]{1,0:T(8,128)}) %reduce-scatter.15.cloned.1.call-update) | async-done | bytes 32784 | tf_op jit(solution)/shard_map/reduce_scatter | solution.py:57
  504.5 1.4 multiply_reduce_fusion.2
  507.1 77.3 %psum.29 = f32[]{:T(128)} all-reduce(f32[]{:T(128)S(6)} %add.92), channel_id=1, replica_groups=mesh['row'=16,'col'=16] {'row','col'}, use_global_device_ids=true, to_apply=%region_9.10 | all-reduce | flops 1 | bytes 8 | tf_op jit(solution)/shard_map/psum | solution.py:37
  585.9 25.4 %all_gather.28 = f32[512,128]{1,0:T(8,128)S(1)} all-gather(f32[32,128]{1,0:T(8,128)S(1)} %divide_subtract_fusion.6), channel_id=1, replica_groups=mesh['row'=16,'col'=16] {'col'}, dimensions={0}, use_global_device_ids=true | all-gather | bytes 278528 | tf_op jit(solution)/shard_map/all_gather | solution.py:50
  611.3 0.8 divide_subtract_fusion.2
  612.1 31.9 %all_gather.29 = f32[1024,128]{1,0:T(8,128)S(1)} all-gather(f32[64,128]{1,0:T(8,128)S(1)} %divide_subtract_fusion.2), channel_id=1, replica_groups=mesh['row'=16,'col'=16] {'row'}, dimensions={0}, use_global_device_ids=true | all-gather | bytes 557056 | tf_op jit(solution)/shard_map/all_gather | solution.py:51
  644.0 6.5 clamp_multiply_fusion.1
  650.6 1.3 copy-done.1
  651.9 2.5 convolution_multiply_fusion.5
  654.5 5.8 convolution_multiply_fusion.1
  660.4 45.9 %reduce-scatter.17.cloned.1.call-done = f32[32,128]{1,0:T(8,128)} async-done(((f32[512,128]{1,0:T(8,128)}), f32[32,128]{1,0:T(8,128)}) %reduce-scatter.17.cloned.1.call-update) | async-done | bytes 16400 | tf_op jit(solution)/shard_map/reduce_scatter | solution.py:54
  706.3 1.3 multiply_reduce_fusion.5
  707.6 84.8 %reduce-scatter.19.cloned.1.call-done = f32[64,128]{1,0:T(8,128)} async-done(((f32[1024,128]{1,0:T(8,128)}), f32[64,128]{1,0:T(8,128)}) %reduce-scatter.19.cloned.1.call-update) | async-done | bytes 32784 | tf_op jit(solution)/shard_map/reduce_scatter | solution.py:57
  792.3 1.4 multiply_reduce_fusion.1
  795.0 77.3 %psum.30 = f32[]{:T(128)} all-reduce(f32[]{:T(128)S(6)} %add.97), channel_id=1, replica_groups=mesh['row'=16,'col'=16] {'row','col'}, use_global_device_ids=true, to_apply=%region_14.15 | all-reduce | flops 1 | bytes 8 | tf_op jit(solution)/shard_map/psum | solution.py:37
  873.8 25.3 %all_gather.30 = f32[512,128]{1,0:T(8,128)S(1)} all-gather(f32[32,128]{1,0:T(8,128)S(1)} %divide_subtract_fusion.5), channel_id=1, replica_groups=mesh['row'=16,'col'=16] {'col'}, dimensions={0}, use_global_device_ids=true | all-gather | bytes 278528 | tf_op jit(solution)/shard_map/all_gather | solution.py:50
  899.0 0.8 divide_subtract_fusion.1
  899.8 32.1 %all_gather.31 = f32[1024,128]{1,0:T(8,128)S(1)} all-gather(f32[64,128]{1,0:T(8,128)S(1)} %divide_subtract_fusion.1), channel_id=1, replica_groups=mesh['row'=16,'col'=16] {'row'}, dimensions={0}, use_global_device_ids=true | all-gather | bytes 557056 | tf_op jit(solution)/shard_map/all_gather | solution.py:51
  931.9 8.5 select_select_fusion
  940.4 1.3 copy-done.2
  941.7 2.5 convolution_multiply_fusion.4
  944.3 5.8 convolution_multiply_fusion
  950.1 46.1 %reduce-scatter.21.cloned.1.call-done = f32[32,128]{1,0:T(8,128)} async-done(((f32[512,128]{1,0:T(8,128)}), f32[32,128]{1,0:T(8,128)}) %reduce-scatter.21.cloned.1.call-update) | async-done | bytes 16400 | tf_op jit(solution)/shard_map/reduce_scatter | solution.py:54
  996.3 1.3 multiply_reduce_fusion.4
  997.6 84.6 %reduce-scatter.23.cloned.1.call-done = f32[64,128]{1,0:T(8,128)} async-done(((f32[1024,128]{1,0:T(8,128)}), f32[64,128]{1,0:T(8,128)}) %reduce-scatter.23.cloned.1.call-update) | async-done | bytes 32784 | tf_op jit(solution)/shard_map/reduce_scatter | solution.py:57
  1082.2 1.4 multiply_reduce_fusion
  1084.9 77.3 %psum.31 = f32[]{:T(128)} all-reduce(f32[]{:T(128)S(6)} %add.102), channel_id=1, replica_groups=mesh['row'=16,'col'=16] {'row','col'}, use_global_device_ids=true, to_apply=%region_19.20 | all-reduce | flops 1 | bytes 8 | tf_op jit(solution)/shard_map/psum | solution.py:37
  1162.9 1.4 divide_subtract_fusion
  1164.2 1.3 divide_subtract_fusion.4
  (26 shorter events, 2.7 us)
Async XLA Ops:
  7.2 123.6 %reduce-scatter.9.cloned.1.call-start = ((), (), s32[]{:S(2)}) async-start(), calls=%async_computation.8 | async-start | bytes 278528 | tf_op jit(solution)/shard_map/reduce_scatter | solution.py:54
  80.7 50.0 %copy-start.4 = (f32[32,128]{1,0:T(8,128)S(1)}, f32[32,128]{1,0:T(8,128)}, u32[]{:S(2)}) copy-start(f32[32,128]{1,0:T(8,128)} %param.8) | copy-start | bytes 49156
  80.7 136.7 %copy-start.3 = (f32[64,128]{1,0:T(8,128)S(1)}, f32[64,128]{1,0:T(8,128)}, u32[]{:S(2)}) copy-start(f32[64,128]{1,0:T(8,128)} %param.9) | copy-start | bytes 98308
  80.7 136.6 %reduce-scatter.11.cloned.1.call-start = ((), (), s32[]{:S(2)}) async-start(), calls=%async_computation.9 | async-start | bytes 557056 | tf_op jit(solution)/shard_map/reduce_scatter | solution.py:57
  85.0 333.6 %reduce-scatter.13.cloned.1.call-start = ((), (), s32[]{:S(2)}) async-start(), calls=%async_computation.10 | async-start | bytes 278528 | tf_op jit(solution)/shard_map/reduce_scatter | solution.py:54
  362.7 1.3 copy-start
  366.5 138.0 %reduce-scatter.15.cloned.1.call-start = ((), (), s32[]{:S(2)}) async-start(), calls=%async_computation.11 | async-start | bytes 557056 | tf_op jit(solution)/shard_map/reduce_scatter | solution.py:57
  372.4 333.9 %reduce-scatter.17.cloned.1.call-start = ((), (), s32[]{:S(2)}) async-start(), calls=%async_computation.12 | async-start | bytes 278528 | tf_op jit(solution)/shard_map/reduce_scatter | solution.py:54
  650.5 1.4 copy-start.1
  654.4 137.9 %reduce-scatter.19.cloned.1.call-start = ((), (), s32[]{:S(2)}) async-start(), calls=%async_computation.13 | async-start | bytes 557056 | tf_op jit(solution)/shard_map/reduce_scatter | solution.py:57
  660.3 336.0 %reduce-scatter.21.cloned.1.call-start = ((), (), s32[]{:S(2)}) async-start(), calls=%async_computation.14 | async-start | bytes 278528 | tf_op jit(solution)/shard_map/reduce_scatter | solution.py:54
  940.4 1.4 copy-start.2
  944.3 137.9 %reduce-scatter.23.cloned.1.call-start = ((), (), s32[]{:S(2)}) async-start(), calls=%async_computation.15 | async-start | bytes 557056 | tf_op jit(solution)/shard_map/reduce_scatter | solution.py:57
Sparse Core Ops, SparseCore 0:
  80.9 49.8 reduce-scatter.8
  135.8 81.4 reduce-scatter.10
  366.6 51.8 reduce-scatter.12
  423.0 81.4 reduce-scatter.14
  654.5 51.6 reduce-scatter.16
  710.6 81.6 reduce-scatter.18
  944.4 51.8 reduce-scatter.20
  1000.8 81.3 reduce-scatter.22
where the time goes:
time: 1170 us
  blocking collectives  547 us (47%)
  waiting for transfers between devices  523 us (45%)
  matrix products  57.5 us (5%)
  between operations  22.2 us (2%)
  other arithmetic  18 us (2%)
    reduce_scatter x4, waiting for transfers between devices, shards(): lax.psum_scatter(col_term, 'row', scatter_dimension=0, tiled=True)  339 us
    psum x4, blocking collectives, norm_scale(): total = lax.psum(local, ('row', 'col'))  309 us
    reduce_scatter x4, waiting for transfers between devices, shards(): lax.psum_scatter(row_term, 'col', scatter_dimension=0, tiled=True)  184 us
    all_gather x4, blocking collectives, shards(): lower_blk = lax.all_gather(lower, 'row', axis=0, tiled=True)  130 us
    all_gather x4, blocking collectives, shards(): upper_blk = lax.all_gather(upper, 'col', axis=0, tiled=True)  108 us
    dot_general x4, matrix products, tile_step(): jnp.dot(upper, lower.T, precision=lax.Precision.HIGHEST, preferred_elemen...  25.8 us
  transfers between devices with their start and end apart: 8, of which 8 were waited for; matrix products, arithmetic and copies ran while one was open for 2% of the time, Pallas kernels for 0%

commit v1 on v0

v1 whole, which is shorter than its diff:
```python
import jax
import jax.numpy as jnp
from jax import lax
from jax.experimental import pallas as pl
from jax.experimental.pallas import tpu as pltpu
from jax.sharding import PartitionSpec as P

ITERS = 4
N = 16
MESH = pl.DeviceIdType.MESH

tau_level = 0.9
rho_penalty = 1.0
lam_reg = 0.1
eta_step = 0.05
eps_norm = 1e-06
LOW = -(1.0 - tau_level) / rho_penalty
HIGH = tau_level / rho_penalty

TILE = 128
F32 = jnp.float32
BF16 = jnp.bfloat16


def split(x):
    hi = x.astype(BF16)
    lo = (x - hi.astype(F32)).astype(BF16)
    return hi, lo


def dot(a, b, dims):
    return lax.dot_general(a, b, (dims, ((), ())), preferred_element_type=F32)


def kernel(count, obs_hbm, mask_hbm, dual_hbm, u0, v0, u_out, v_out, state_hbm,
           obs, mask, state, ub, vb, gub, gvb, ucat, vcat, chi, clo, pu, pv, ru, rv,
           n1, n2, ss, rs, ls):
    row = lax.axis_index("row")
    col = lax.axis_index("col")
    ns, ms = u0.shape[0], v0.shape[0]
    nr, nc = obs.shape
    rank = u0.shape[1]

    loads = [pltpu.make_async_copy(a, b, ls.at[i])
             for i, (a, b) in enumerate(((obs_hbm, obs), (mask_hbm, mask), (dual_hbm, state)))]
    for c in loads:
        c.start()

    def along_col(k):
        return (row, lax.rem(col + k, N))

    def along_row(k):
        return (lax.rem(row + k, N), col)

    bar = pltpu.get_barrier_semaphore()
    for k in range(1, N):
        pl.semaphore_signal(bar, inc=1, device_id=along_col(k), device_id_type=MESH)
        pl.semaphore_signal(bar, inc=1, device_id=along_row(k), device_id_type=MESH)
    pl.semaphore_wait(bar, 2 * (N - 1))

    def send(src, dst, i, to):
        pltpu.make_async_remote_copy(
            src_ref=src, dst_ref=dst, send_sem=ss.at[i], recv_sem=rs.at[i],
            device_id=to, device_id_type=MESH).start()

    def wait(ref, sem):
        pltpu.make_async_copy(ref, ref, sem).wait()

    own_u = pl.ds(pl.multiple_of(col * ns, ns), ns)
    own_v = pl.ds(pl.multiple_of(row * ms, ms), ms)
    most_u = pl.ds(0, (N - 1) * ns)
    most_v = pl.ds(0, (N - 1) * ms)

    for k in range(1, N):
        send(v0, vb.at[own_v], 1, along_row(k))
        send(u0, ub.at[own_u], 0, along_col(k))
    ub[own_u, :] = u0[...]
    vb[own_v, :] = v0[...]
    for c in loads:
        c.wait()
    for i, ref in ((0, ub.at[most_u]), (1, vb.at[most_v])):
        wait(ref, rs.at[i])
        wait(ref, ss.at[i])

    def sweep(t, carry):
        uh, ul = split(ub[...])
        ucat[:, :rank] = uh
        ucat[:, rank:] = ul
        vh, vl = split(vb[...])
        vcat[:, :rank] = vh
        vcat[:, rank:] = vl

        @pl.loop(0, nr // TILE)
        def _(i):
            rows = pl.ds(pl.multiple_of(i * TILE, TILE), TILE)
            a = ucat[rows, :]
            vh = vcat[:, :rank]
            pred = dot(a, jnp.concatenate([vh, vh], axis=1), ((1,), (1,)))
            pred += dot(a[:, :rank], vcat[:, rank:], ((1,), (1,)))
            old = state[rows, :]
            wide = obs[rows, :] - pred + old / rho_penalty
            c = jnp.clip(wide, LOW, HIGH)
            on = mask[rows, :] == 1
            state[rows, :] = jnp.where(on, rho_penalty * c, old)
            hi, lo = split(jnp.where(on, c, 0.0))
            chi[rows, :] = hi
            clo[rows, :] = lo

        @pl.loop(0, nr // TILE)
        def _(i):
            rows = pl.ds(pl.multiple_of(i * TILE, TILE), TILE)
            both = jnp.concatenate([chi[rows, :], clo[rows, :]], axis=0)
            g = dot(both, vcat[...], ((1,), (0,)))
            g = g[:TILE] + g[TILE:]
            pu[rows, :] = -rho_penalty * (g[:, :rank] + g[:, rank:])

        for k in range(1, N):
            to = lax.rem(col + k, N)
            send(pu.at[pl.ds(pl.multiple_of(to * ns, ns), ns)], ru.at[k - 1], 2, along_col(k))

        for j in range(nc // 256):
            cols = slice(j * 256, (j + 1) * 256)
            g = dot(chi[:, cols], ucat[...], ((0,), (0,))) + dot(clo[:, cols], ucat[...], ((0,), (0,)))
            pv[cols, :] = -rho_penalty * (g[:, :rank] + g[:, rank:])

        for k in range(1, N):
            to = lax.rem(row + k, N)
            send(pv.at[pl.ds(pl.multiple_of(to * ms, ms), ms)], rv.at[k - 1], 3, along_row(k))

        last = t == ITERS - 1

        wait(ru, rs.at[2])
        gu = pu[own_u, :] + jnp.sum(ru[...], axis=0) + lam_reg * ub[own_u, :]
        gub[own_u, :] = gu

        @pl.when(jnp.logical_not(last))
        def _():
            for k in range(1, N):
                send(gub.at[own_u], gub.at[own_u], 0, along_col(k))

        wait(rv, rs.at[3])
        gv = pv[own_v, :] + jnp.sum(rv[...], axis=0) + lam_reg * vb[own_v, :]
        gvb[own_v, :] = gv
        part = jnp.sum((gu * gu).reshape(ns // 8, 8, rank), axis=0)
        n1[N - 1] = part + jnp.sum((gv * gv).reshape(ms // 8, 8, rank), axis=0)
        for k in range(1, N):
            send(n1.at[N - 1], n1.at[k - 1], 4, along_col(k))

        @pl.when(jnp.logical_not(last))
        def _():
            for k in range(1, N):
                send(gvb.at[own_v], gvb.at[own_v], 1, along_row(k))

        wait(n1.at[pl.ds(0, N - 1)], rs.at[4])
        n2[N - 1] = jnp.sum(n1[...], axis=0)
        for k in range(1, N):
            send(n2.at[N - 1], n2.at[k - 1], 5, along_row(k))
        wait(n2.at[pl.ds(0, N - 1)], rs.at[5])
        total = jnp.sum(n2[...], axis=(0, 1, 2), keepdims=True)[0]
        scale = jnp.sqrt(total / count + eps_norm)

        @pl.when(jnp.logical_not(last))
        def _():
            for i, ref, g, full in ((0, gub.at[most_u], gub, ub), (1, gvb.at[most_v], gvb, vb)):
                wait(ref, rs.at[i])
                wait(ref, ss.at[i])
                full[...] = full[...] - eta_step * g[...] / scale

        @pl.when(last)
        def _():
            u_out[...] = ub[own_u, :] - eta_step * gub[own_u, :] / scale
            v_out[...] = vb[own_v, :] - eta_step * gvb[own_v, :] / scale

        wait(ru, ss.at[2])
        wait(rv, ss.at[3])
        wait(n1.at[pl.ds(0, N - 1)], ss.at[4])
        wait(n2.at[pl.ds(0, N - 1)], ss.at[5])
        return carry

    lax.fori_loop(0, ITERS, sweep, 0)
    out = pltpu.make_async_copy(state, state_hbm, ls.at[0])
    out.start()
    out.wait()


def shards(observed, mask, dual, row_factor, col_factor):
    nr, nc = observed.shape
    ns, rank = row_factor.shape
    ms = col_factor.shape[0]
    count = (nr + nc) * N * rank

    def body(*refs):
        kernel(count, *refs)

    vmem = pl.BlockSpec(memory_space=pltpu.VMEM)
    hbm = pl.BlockSpec(memory_space=pl.ANY)
    return pl.pallas_call(
        body,
        out_shape=(
            jax.ShapeDtypeStruct((ns, rank), F32),
            jax.ShapeDtypeStruct((ms, rank), F32),
            jax.ShapeDtypeStruct((nr, nc), F32),
        ),
        in_specs=[hbm, hbm, hbm, vmem, vmem],
        out_specs=(vmem, vmem, hbm),
        scratch_shapes=[
            pltpu.VMEM((nr, nc), F32),
            pltpu.VMEM((nr, nc), jnp.int32),
            pltpu.VMEM((nr, nc), F32),
            pltpu.VMEM((nr, rank), F32),
            pltpu.VMEM((nc, rank), F32),
            pltpu.VMEM((nr, rank), F32),
            pltpu.VMEM((nc, rank), F32),
            pltpu.VMEM((nr, 2 * rank), BF16),
            pltpu.VMEM((nc, 2 * rank), BF16),
            pltpu.VMEM((nr, nc), BF16),
            pltpu.VMEM((nr, nc), BF16),
            pltpu.VMEM((nr, rank), F32),
            pltpu.VMEM((nc, rank), F32),
            pltpu.VMEM((N - 1, ns, rank), F32),
            pltpu.VMEM((N - 1, ms, rank), F32),
            pltpu.VMEM((N, 8, rank), F32),
            pltpu.VMEM((N, 8, rank), F32),
            pltpu.SemaphoreType.DMA((6,)),
            pltpu.SemaphoreType.DMA((6,)),
            pltpu.SemaphoreType.DMA((3,)),
        ],
        compiler_params=pltpu.CompilerParams(
            collective_id=0, has_side_effects=True, vmem_limit_bytes=48 * 1024 * 1024
        ),
        cost_estimate=pl.CostEstimate(
            flops=ITERS * 6 * nr * nc * rank, bytes_accessed=16 * nr * nc, transcendentals=0
        ),
        name="admm_sweeps",
    )(observed, mask, dual, row_factor, col_factor)


def solution(mesh):
    in_specs = (
        P("row", "col"),
        P("row", "col"),
        P("row", "col"),
        P(("row", "col"), None),
        P(("col", "row"), None),
    )
    out_specs = (P(("row", "col"), None), P(("col", "row"), None), P("row", "col"))
    return jax.shard_map(shards, mesh=mesh, in_specs=in_specs, out_specs=out_specs, check_vma=False)
```

time: 1170 us -> 138 us (0.12)
  blocking collectives: 547 us -> 0 us
  waiting for transfers between devices: 523 us -> 0 us
  Pallas kernels: 0 us -> 132 us
  matrix products: 57.5 us -> 0 us
  between operations: 22.2 us -> 0.65 us
  other arithmetic: 18 us -> 0 us
    reduce_scatter x8 -> x0, waiting for transfers between devices: 523 us -> none  [the longest x4 339 us: shards(): lax.psum_scatter(col_term, 'row', scatter_dimension=0, tiled=True)]
    psum x4 -> x0, blocking collectives: 309 us -> none  [norm_scale(): total = lax.psum(local, ('row', 'col'))]
    all_gather x8 -> x0, blocking collectives: 238 us -> none  [the longest x4 130 us: shards(): lower_blk = lax.all_gather(lower, 'row', axis=0, tiled=True)]
    pallas_call x0 -> x1, Pallas kernels: none -> 132 us  [shards(): pl.pallas_call(body, out_shape=(jax.ShapeDtypeStruct((ns, rank), F32), ja...]
    dot_general x12 -> x0, matrix products: 57.5 us -> none  [the longest x4 25.8 us: tile_step(): jnp.dot(upper, lower.T, precision=lax.Precision.HIGHEST, preferred_elemen...]
  transfers between devices with their start and end apart: 8 -> 0, of which waited for: 8 -> 0; matrix products, arithmetic and copies ran while one was open for 2% -> 0% of each run, Pallas kernels for 0% -> 0%
where the time goes in v1:
time: 138 us
  Pallas kernels  132 us (96%)
  local copies, waits for them, and re-layouts  5.6 us (4%)
    pallas_call x1, Pallas kernels, shards(): pl.pallas_call(body, out_shape=(jax.ShapeDtypeStruct((ns, rank), F32), ja...  132 us
    unnamed x9, local copies, waits for them, and re-layouts  5.6 us

profile of v1, /device:TPU:1, one launch (start us, length us, event | category | flops | bytes accessed | tf_op | source)
XLA Modules:
  0.0 138.0 jit_solution(11785716307621678473)
XLA Ops:
  0.6 0.0 copy-start
  0.6 1.6 %copy-done = f32[512,1024]{1,0:T(8,128)S(1)} copy-done((f32[512,1024]{1,0:T(8,128)S(1)}, f32[512,1024]{1,0:T(8,128)}, u32[]{:S(2)}) %copy-start) | copy-done | bytes 2097176
  2.2 0.0 copy-start.1
  2.2 0.8 copy-done.1
  3.0 0.0 copy-start.2
  3.0 0.7 copy-done.2
  3.7 131.7 %admm_sweeps.1 = (f32[32,128]{1,0:T(8,128)S(1)}, f32[64,128]{1,0:T(8,128)S(1)}, f32[512,1024]{1,0:T(8,128)S(1)}) custom-call(f32[512,1024]{1,0:T(8,128)S(1)} %copy-done, s32[512,1024]{1,0:T(8,128)} %refs_1_.1, f32[512,1024]{1,0:T(8,128)} %refs_2_.1, f32[32,128]{1,0:T(8,128)S(1)} %copy-done.2, f32[64,128]{1,0:T(8,128)S(1)} %copy-done.1), custom_call_target="tpu_custom_call" | custom-call | flops 1610612736 | bytes 8388608 | tf_op jit(solution)/shard_map/admm_sweeps/pallas_call | solution.py:197
  135.4 0.6 copy.11
  136.0 0.6 copy.12
  136.6 1.3 copy.13
Async XLA Ops:
  0.6 1.6 %copy-start = (f32[512,1024]{1,0:T(8,128)S(1)}, f32[512,1024]{1,0:T(8,128)}, u32[]{:S(2)}) copy-start(f32[512,1024]{1,0:T(8,128)} %refs_0_.1) | copy-start | bytes 6291460
  2.2 0.8 copy-start.1
  3.0 0.7 copy-start.2

commit v2 on v1

v2 whole, which is shorter than its diff:
```python
import jax
import jax.numpy as jnp
from jax import lax
from jax.experimental import pallas as pl
from jax.experimental.pallas import tpu as pltpu
from jax.sharding import PartitionSpec as P

ITERS = 4
N = 16
MESH = pl.DeviceIdType.MESH

tau_level = 0.9
rho_penalty = 1.0
lam_reg = 0.1
eta_step = 0.05
eps_norm = 1e-06
LOW = -(1.0 - tau_level) / rho_penalty
HIGH = tau_level / rho_penalty

TILE = 128
FAR_COL = (9, 8, 7, 6, 10, 5, 11, 4, 12, 3, 13, 2, 14, 1, 15)
FAR_ROW = (10, 8, 6, 11, 7, 9, 5, 14, 12, 2, 4, 3, 13, 15, 1)
FAR_CHIP = ((2, 1), (1, 1), (3, 1), (2, 0), (0, 1), (1, 0), (3, 0))
F32 = jnp.float32
BF16 = jnp.bfloat16


def split(x):
    hi = x.astype(BF16)
    lo = (x - hi.astype(F32)).astype(BF16)
    return hi, lo


def dot(a, b, dims):
    return lax.dot_general(a, b, (dims, ((), ())), preferred_element_type=F32)


def kernel(count, obs_hbm, mask_hbm, dual_hbm, u0, v0, u_out, v_out, state_hbm,
           obs, mask, state, ub, vb, gub, gvb, ucat, vcat, chi, clo, pu, pv, sib, ru, rv,
           nb, load, out, us, ur, vs, vr, fs, fr, pus, pur, bs, br, pvs, pvr, nss, nsr):
    row = lax.axis_index("row")
    col = lax.axis_index("col")
    z, xlo = col // 2, lax.rem(col, 2)
    y, xhi, core = row // 4, lax.rem(row // 2, 2), lax.rem(row, 2)
    chip = row // 2
    nr, nc = obs.shape
    ns, ms = nr // N, nc // N
    rank = ub.shape[1]
    sibling = (row + 1 - 2 * core, col)

    own_u = pl.ds(pl.multiple_of(col * ns, ns), ns)
    loads = [pltpu.make_async_copy(a, b, load.at[i])
             for i, (a, b) in enumerate(((u0, ub.at[own_u]), (v0, vb.at[chip, core]),
                                         (obs_hbm, obs), (mask_hbm, mask), (dual_hbm, state)))]
    for c in loads:
        c.start()

    bar = pltpu.get_barrier_semaphore()
    for k in FAR_COL:
        pl.semaphore_signal(bar, inc=1, device_id=(row, lax.rem(col + k, N)), device_id_type=MESH)
    for k in FAR_ROW:
        pl.semaphore_signal(bar, inc=1, device_id=(lax.rem(row + k, N), col), device_id_type=MESH)
    pl.semaphore_wait(bar, 2 * (N - 1))

    def send(src, dst, ss, rs, to):
        pltpu.make_async_remote_copy(
            src_ref=src, dst_ref=dst, send_sem=ss, recv_sem=rs,
            device_id=to, device_id_type=MESH).start()

    def wait(ref, sem):
        pltpu.make_async_copy(ref, ref, sem).wait()

    def chip_at(dy, dx):
        return lax.rem(y + dy, 4) * 2 + (1 - xhi if dx else xhi)

    def gather_u(dst):
        for k in FAR_COL:
            send(dst.at[own_u], dst.at[own_u], us, ur, (row, lax.rem(col + k, N)))

    def gather_v(dst):
        own = dst.at[chip, core]
        for i, (dy, dx) in enumerate(FAR_CHIP):
            send(own, own, vs, vr.at[i], (chip_at(dy, dx) * 2 + core, col))
        send(own, own, fs, fr, sibling)

    def forward_v(dst):
        for i, (dy, dx) in reversed(list(enumerate(FAR_CHIP))):
            got = dst.at[chip_at(4 - dy, dx), core]
            wait(got, vr.at[i])
            send(got, got, fs, fr, sibling)

    def gathered_u(dst):
        most = dst.at[pl.ds(0, (N - 1) * ns)]
        wait(most, ur)
        wait(most, us)

    def gathered_v(dst):
        wait(dst.at[:, 0], fr)
        wait(dst.at[pl.ds(0, 7), 0], vs)
        wait(dst.at[:, 0], fs)

    loads[0].wait()
    gather_u(ub)
    loads[1].wait()
    gather_v(vb)
    forward_v(vb)
    for c in loads[2:]:
        c.wait()
    gathered_v(vb)
    gathered_u(ub)

    def sweep(t, carry):
        last = t == ITERS - 1
        uh, ul = split(ub[...])
        ucat[:, :rank] = uh
        ucat[:, rank:] = ul
        vh, vl = split(vb[...].reshape(nc, rank))
        vcat[:, :rank] = vh
        vcat[:, rank:] = vl

        for dm in (2, 1, 3, 0):
            m = lax.rem(z // 2 + dm, 4)
            rows = pl.ds(pl.multiple_of(m * TILE, TILE), TILE)
            a = ucat[rows, :]
            vh = vcat[:, :rank]
            pred = dot(a, jnp.concatenate([vh, vh], axis=1), ((1,), (1,)))
            pred += dot(a[:, :rank], vcat[:, rank:], ((1,), (1,)))
            old = state[rows, :]
            wide = obs[rows, :] - pred + old / rho_penalty
            c = jnp.clip(wide, LOW, HIGH)
            on = mask[rows, :] == 1
            state[rows, :] = jnp.where(on, rho_penalty * c, old)
            hi, lo = split(jnp.where(on, c, 0.0))
            chi[rows, :] = hi
            clo[rows, :] = lo
            g = dot(jnp.concatenate([hi, lo], axis=0), vcat[...], ((1,), (0,)))
            g = g[:TILE] + g[TILE:]
            pu[rows, :] = -rho_penalty * (g[:, :rank] + g[:, rank:])
            for i in range(4):
                if dm == 0 and i == 0:
                    continue
                to = 4 * m + lax.rem(lax.rem(col, 4) + i, 4)
                src = pu.at[pl.ds(pl.multiple_of(to * ns, ns), ns)]
                send(src, ru.at[col], pus, pur, (row, to))
        ru[col] = pu[own_u, :]

        @pl.when(last)
        def _():
            pltpu.make_async_copy(state, state_hbm, out).start()

        def part_v(i, dy):
            yy = lax.rem(y + dy, 4)
            cols = pl.ds(pl.multiple_of(yy * 256, 256), 256)
            u = ucat[...]
            g = dot(chi[:, cols], u, ((0,), (0,))) + dot(clo[:, cols], u, ((0,), (0,)))
            g = -rho_penalty * (g[:, :rank] + g[:, rank:])
            for hi in range(2):
                for co in range(2):
                    pv[yy, co, hi] = g[(2 * hi + co) * ms:(2 * hi + co + 1) * ms]
            send(pv.at[yy, 1 - core], sib.at[yy], bs, br.at[i], sibling)

        def send_v(i, dy):
            yy = lax.rem(y + dy, 4)
            wait(sib.at[yy], br.at[i])
            pv[yy, core] = pv[yy, core] + sib[yy]
            for dx in (1, 0):
                if dy == 0 and dx == 0:
                    continue
                ch = chip_at(dy, dx)
                hi = 1 - xhi if dx else xhi
                send(pv.at[yy, core, hi], rv.at[chip], pvs, pvr, (ch * 2 + core, col))

        order = (2, 1, 3, 0)
        for i, dy in enumerate(order):
            part_v(i, dy)
            if i:
                send_v(i - 1, order[i - 1])
        send_v(3, 0)
        rv[chip] = pv[y, core, xhi]

        wait(ru.at[pl.ds(0, N - 1)], pur)
        gu = jnp.sum(ru[...], axis=0) + lam_reg * ub[own_u, :]
        gub[own_u, :] = gu

        @pl.when(jnp.logical_not(last))
        def _():
            gather_u(gub)

        wait(rv.at[pl.ds(0, 7)], pvr)
        gv = jnp.sum(rv[...], axis=0) + lam_reg * vb[chip, core]
        gvb[chip, core] = gv

        @pl.when(jnp.logical_not(last))
        def _():
            gather_v(gvb)

        par = lax.rem(t, 2)
        me = row * N + col
        part = jnp.sum(gu * gu, axis=0, keepdims=True) + jnp.sum(gv * gv, axis=0, keepdims=True)
        mine = nb.at[par, pl.ds(me, 1)]
        nb[par, pl.ds(me, 1), :] = part
        for dz in (4, 3, 5, 2, 6, 1, 7, 0):
            zz = lax.rem(z + dz, 8)

            def one(e, carry):
                xx = lax.rem(xlo + lax.rem(e, 2), 2)
                to = (lax.rem(row + e // 2, N), zz * 2 + xx)
                send(mine, mine, nss, nsr.at[par], to)
                return carry

            lax.fori_loop(0 if dz else 1, 2 * N, one, 0)

        @pl.when(jnp.logical_not(last))
        def _():
            forward_v(gvb)

        wait(nb.at[par, pl.ds(0, N * N - 1)], nsr.at[par])
        total = jnp.sum(nb[par], axis=(0, 1), keepdims=True)
        step = eta_step / jnp.sqrt(total / count + eps_norm)

        @pl.when(jnp.logical_not(last))
        def _():
            gathered_u(gub)
            ub[...] = ub[...] - step * gub[...]
            gathered_v(gvb)
            vb[...] = vb[...] - step * gvb[...]

        @pl.when(last)
        def _():
            u_out[...] = ub[own_u, :] - step * gub[own_u, :]
            v_out[...] = vb[chip, core] - step * gvb[chip, core]
            pltpu.make_async_copy(state, state_hbm, out).wait()

        wait(ru.at[pl.ds(0, N - 1)], pus)
        wait(rv.at[pl.ds(0, 7)], pvs)
        wait(sib, bs)
        wait(nb.at[par, pl.ds(0, N * N - 1)], nss)
        return carry

    lax.fori_loop(0, ITERS, sweep, 0)


def shards(observed, mask, dual, row_factor, col_factor):
    nr, nc = observed.shape
    ns, rank = row_factor.shape
    ms = col_factor.shape[0]
    count = (nr + nc) * N * rank

    def body(*refs):
        kernel(count, *refs)

    vmem = pl.BlockSpec(memory_space=pltpu.VMEM)
    hbm = pl.BlockSpec(memory_space=pl.ANY)
    return pl.pallas_call(
        body,
        out_shape=(
            jax.ShapeDtypeStruct((ns, rank), F32),
            jax.ShapeDtypeStruct((ms, rank), F32),
            jax.ShapeDtypeStruct((nr, nc), F32),
        ),
        in_specs=[hbm] * 5,
        out_specs=(vmem, vmem, hbm),
        scratch_shapes=[
            pltpu.VMEM((nr, nc), F32),
            pltpu.VMEM((nr, nc), jnp.int32),
            pltpu.VMEM((nr, nc), F32),
            pltpu.VMEM((nr, rank), F32),
            pltpu.VMEM((8, 2, ms, rank), F32),
            pltpu.VMEM((nr, rank), F32),
            pltpu.VMEM((8, 2, ms, rank), F32),
            pltpu.VMEM((nr, 2 * rank), BF16),
            pltpu.VMEM((nc, 2 * rank), BF16),
            pltpu.VMEM((nr, nc), BF16),
            pltpu.VMEM((nr, nc), BF16),
            pltpu.VMEM((nr, rank), F32),
            pltpu.VMEM((4, 2, 2, ms, rank), F32),
            pltpu.VMEM((4, 2, ms, rank), F32),
            pltpu.VMEM((N, ns, rank), F32),
            pltpu.VMEM((8, ms, rank), F32),
            pltpu.VMEM((2, N * N, rank), F32),
            pltpu.SemaphoreType.DMA((5,)),
            pltpu.SemaphoreType.DMA,
            pltpu.SemaphoreType.DMA,
            pltpu.SemaphoreType.DMA,
            pltpu.SemaphoreType.DMA,
            pltpu.SemaphoreType.DMA((7,)),
            pltpu.SemaphoreType.DMA,
            pltpu.SemaphoreType.DMA,
            pltpu.SemaphoreType.DMA,
            pltpu.SemaphoreType.DMA,
            pltpu.SemaphoreType.DMA,
            pltpu.SemaphoreType.DMA((4,)),
            pltpu.SemaphoreType.DMA,
            pltpu.SemaphoreType.DMA,
            pltpu.SemaphoreType.DMA,
            pltpu.SemaphoreType.DMA((2,)),
        ],
        compiler_params=pltpu.CompilerParams(
            collective_id=0, has_side_effects=True, vmem_limit_bytes=60 * 1024 * 1024
        ),
        cost_estimate=pl.CostEstimate(
            flops=ITERS * 6 * nr * nc * rank, bytes_accessed=16 * nr * nc, transcendentals=0
        ),
        name="admm_sweeps",
    )(observed, mask, dual, row_factor, col_factor)


def solution(mesh):
    in_specs = (
        P("row", "col"),
        P("row", "col"),
        P("row", "col"),
        P(("row", "col"), None),
        P(("col", "row"), None),
    )
    out_specs = (P(("row", "col"), None), P(("col", "row"), None), P("row", "col"))
    return jax.shard_map(shards, mesh=mesh, in_specs=in_specs, out_specs=out_specs, check_vma=False)
```

time: 138 us -> 119 us (0.86)
  Pallas kernels: 132 us -> 112 us
    pallas_call x1, Pallas kernels: 132 us -> 112 us  [shards(): pl.pallas_call(body, out_shape=(jax.ShapeDtypeStruct((ns, rank), F32), ja...]
    unnamed x9 -> x3, local copies, waits for them, and re-layouts: 5.6 us -> 5.86 us
where the time goes in v2:
time: 119 us
  Pallas kernels  112 us (94%)
  local copies, waits for them, and re-layouts  5.86 us (5%)
    pallas_call x1, Pallas kernels, shards(): pl.pallas_call(body, out_shape=(jax.ShapeDtypeStruct((ns, rank), F32), ja...  112 us
    unnamed x3, local copies, waits for them, and re-layouts  5.86 us

profile of v2, /device:TPU:1, one launch (start us, length us, event | category | flops | bytes accessed | tf_op | source)
XLA Modules:
  0.0 118.8 jit_solution(16416025337129787888)
XLA Ops:
  0.6 112.3 %admm_sweeps.1 = (f32[32,128]{1,0:T(8,128)}, f32[64,128]{1,0:T(8,128)}, f32[512,1024]{1,0:T(8,128)}) custom-call(f32[512,1024]{1,0:T(8,128)} %refs_0_.1, s32[512,1024]{1,0:T(8,128)} %refs_1_.1, f32[512,1024]{1,0:T(8,128)} %refs_2_.1, f32[32,128]{1,0:T(8,128)} %refs_3_.1, f32[64,128]{1,0:T(8,128)} %refs_4_.1), custom_call_target="tpu_custom_call" | custom-call | flops 1610612736 | bytes 8388608 | tf_op jit(solution)/shard_map/admm_sweeps/pallas_call | solution.py:254
  113.0 1.3 %copy.11 = f32[32,128]{1,0:T(8,128)} copy(f32[32,128]{1,0:T(8,128)} %get-tuple-element.6) | data formatting | bytes 32768
  114.3 1.4 %copy.12 = f32[64,128]{1,0:T(8,128)} copy(f32[64,128]{1,0:T(8,128)} %get-tuple-element.7) | data formatting | bytes 65536
  115.7 3.2 %copy.13 = f32[512,1024]{1,0:T(8,128)} copy(f32[512,1024]{1,0:T(8,128)} %get-tuple-element.8) | data formatting | bytes 4194304

commit v3 on v2

--- a/solution.py
+++ b/solution.py
@@ -20,6 +20,10 @@
 TILE = 128
 FAR_COL = (9, 8, 7, 6, 10, 5, 11, 4, 12, 3, 13, 2, 14, 1, 15)
 FAR_ROW = (10, 8, 6, 11, 7, 9, 5, 14, 12, 2, 4, 3, 13, 15, 1)
+FAR_PLANE = sorted(
+    ((dy, dx, dc) for dy in range(4) for dx in range(4) for dc in range(2)),
+    key=lambda d: -min(d[0], 4 - d[0]) * 4 - min(d[1], 4 - d[1]) * 4 - d[2],
+)
 FAR_CHIP = ((2, 1), (1, 1), (3, 1), (2, 0), (0, 1), (1, 0), (3, 0))
 F32 = jnp.float32
 BF16 = jnp.bfloat16
@@ -35,14 +39,17 @@
     return lax.dot_general(a, b, (dims, ((), ())), preferred_element_type=F32)
 
 
-def kernel(count, obs_hbm, mask_hbm, dual_hbm, u0, v0, u_out, v_out, state_hbm,
-           obs, mask, state, ub, vb, gub, gvb, ucat, vcat, chi, clo, pu, pv, sib, ru, rv,
-           nb, load, out, us, ur, vs, vr, fs, fr, pus, pur, bs, br, pvs, pvr, nss, nsr):
+def kernel(count, obs_hbm, mask_hbm, dual_hbm, u0, v0, u_out, v_out, state,
+           obs, mask, ub, vb, gub, gvb, ucat, vcat, chi, clo, pu, pv, sib, ru, rv,
+           nb, load, us, ur, vs, vr, fs, fr, pus, pur, bs, br, pvs, pvr, nss, nsr):
     row = lax.axis_index("row")
     col = lax.axis_index("col")
     z, xlo = col // 2, lax.rem(col, 2)
     y, xhi, core = row // 4, lax.rem(row // 2, 2), lax.rem(row, 2)
     chip = row // 2
+    ys = [lax.rem(y + d, 4) for d in range(4)]
+    xs = [(lax.rem(xhi * 2 + xlo + d, 4) // 2, lax.rem(xlo + d, 2)) for d in range(4)]
+    cores = (core, 1 - core)
     nr, nc = obs.shape
     ns, ms = nr // N, nc // N
     rank = ub.shape[1]
@@ -144,10 +151,6 @@
                 send(src, ru.at[col], pus, pur, (row, to))
         ru[col] = pu[own_u, :]
 
-        @pl.when(last)
-        def _():
-            pltpu.make_async_copy(state, state_hbm, out).start()
-
         def part_v(i, dy):
             yy = lax.rem(y + dy, 4)
             cols = pl.ds(pl.multiple_of(yy * 256, 256), 256)
@@ -199,16 +202,18 @@
         part = jnp.sum(gu * gu, axis=0, keepdims=True) + jnp.sum(gv * gv, axis=0, keepdims=True)
         mine = nb.at[par, pl.ds(me, 1)]
         nb[par, pl.ds(me, 1), :] = part
-        for dz in (4, 3, 5, 2, 6, 1, 7, 0):
-            zz = lax.rem(z + dz, 8)
-
-            def one(e, carry):
-                xx = lax.rem(xlo + lax.rem(e, 2), 2)
-                to = (lax.rem(row + e // 2, N), zz * 2 + xx)
-                send(mine, mine, nss, nsr.at[par], to)
-                return carry
-
-            lax.fori_loop(0 if dz else 1, 2 * N, one, 0)
+        def tell(zz, skip):
+            for dy, dx, dc in FAR_PLANE[:len(FAR_PLANE) - skip]:
+                send(mine, mine, nss, nsr.at[par],
+                     (ys[dy] * 4 + xs[dx][0] * 2 + cores[dc], zz * 2 + xs[dx][1]))
+
+        def layer(i, carry):
+            dz = 4 + (i + 1) // 2 * (1 - 2 * lax.rem(i, 2))
+            tell(lax.rem(z + dz, 8), 0)
+            return carry
+
+        lax.fori_loop(0, 7, layer, 0)
+        tell(z, 1)
 
         @pl.when(jnp.logical_not(last))
         def _():
@@ -229,7 +234,6 @@
         def _():
             u_out[...] = ub[own_u, :] - step * gub[own_u, :]
             v_out[...] = vb[chip, core] - step * gvb[chip, core]
-            pltpu.make_async_copy(state, state_hbm, out).wait()
 
         wait(ru.at[pl.ds(0, N - 1)], pus)
         wait(rv.at[pl.ds(0, 7)], pvs)
@@ -240,6 +244,15 @@
     lax.fori_loop(0, ITERS, sweep, 0)
 
 
+def hand_out(a0, a1, a2, b0, b1, b2, sem):
+    copies = [pltpu.make_async_copy(a, b, sem.at[i])
+              for i, (a, b) in enumerate(((a2, b2), (a0, b0), (a1, b1)))]
+    for c in copies:
+        c.start()
+    for c in copies:
+        c.wait()
+
+
 def shards(observed, mask, dual, row_factor, col_factor):
     nr, nc = observed.shape
     ns, rank = row_factor.shape
@@ -250,20 +263,19 @@
         kernel(count, *refs)
 
     vmem = pl.BlockSpec(memory_space=pltpu.VMEM)
-    hbm = pl.BlockSpec(memory_space=pl.ANY)
-    return pl.pallas_call(
+    hbm = pl.BlockSpec(memory_space=pltpu.HBM)
+    outs = pl.pallas_call(
         body,
         out_shape=(
-            jax.ShapeDtypeStruct((ns, rank), F32),
-            jax.ShapeDtypeStruct((ms, rank), F32),
-            jax.ShapeDtypeStruct((nr, nc), F32),
+            pltpu.VMEM((ns, rank), F32),
+            pltpu.VMEM((ms, rank), F32),
+            pltpu.VMEM((nr, nc), F32),
         ),
         in_specs=[hbm] * 5,
-        out_specs=(vmem, vmem, hbm),
+        out_specs=(vmem, vmem, vmem),
         scratch_shapes=[
             pltpu.VMEM((nr, nc), F32),
             pltpu.VMEM((nr, nc), jnp.int32),
-            pltpu.VMEM((nr, nc), F32),
             pltpu.VMEM((nr, rank), F32),
             pltpu.VMEM((8, 2, ms, rank), F32),
             pltpu.VMEM((nr, rank), F32),
@@ -282,7 +294,6 @@
             pltpu.SemaphoreType.DMA,
             pltpu.SemaphoreType.DMA,
             pltpu.SemaphoreType.DMA,
-            pltpu.SemaphoreType.DMA,
             pltpu.SemaphoreType.DMA((7,)),
             pltpu.SemaphoreType.DMA,
             pltpu.SemaphoreType.DMA,
@@ -296,13 +307,14 @@
             pltpu.SemaphoreType.DMA((2,)),
         ],
         compiler_params=pltpu.CompilerParams(
-            collective_id=0, has_side_effects=True, vmem_limit_bytes=60 * 1024 * 1024
+            collective_id=0, has_side_effects=True, vmem_limit_bytes=58 * 1024 * 1024
         ),
         cost_estimate=pl.CostEstimate(
             flops=ITERS * 6 * nr * nc * rank, bytes_accessed=16 * nr * nc, transcendentals=0
         ),
         name="admm_sweeps",
     )(observed, mask, dual, row_factor, col_factor)
+    return outs
 
 
 def solution(mesh):

time: 119 us -> 113 us (0.950)
  local copies, waits for them, and re-layouts: 5.86 us -> 2.54 us
  Pallas kernels: 112 us -> 109 us
    unnamed x3, local copies, waits for them, and re-layouts: 5.86 us -> 2.54 us
    pallas_call x1, Pallas kernels: 112 us -> 109 us  [shards(): pl.pallas_call(body, out_shape=(pltpu.VMEM((ns, rank), F32), pltpu.VMEM((...]
where the time goes in v3:
time: 113 us
  Pallas kernels  109 us (96%)
  local copies, waits for them, and re-layouts  2.54 us (2%)
    pallas_call x1, Pallas kernels, shards(): pl.pallas_call(body, out_shape=(pltpu.VMEM((ns, rank), F32), pltpu.VMEM((...  109 us
    unnamed x3, local copies, waits for them, and re-layouts  2.54 us

profile of v3, /device:TPU:1, one launch (start us, length us, event | category | flops | bytes accessed | tf_op | source)
XLA Modules:
  0.0 112.6 jit_solution(15325206849971894957)
XLA Ops:
  0.6 109.4 %admm_sweeps.1 = (f32[32,128]{1,0:T(8,128)S(1)}, f32[64,128]{1,0:T(8,128)S(1)}, f32[512,1024]{1,0:T(8,128)S(1)}) custom-call(f32[512,1024]{1,0:T(8,128)} %refs_0_.1, s32[512,1024]{1,0:T(8,128)} %refs_1_.1, f32[512,1024]{1,0:T(8,128)} %refs_2_.1, f32[32,128]{1,0:T(8,128)} %refs_3_.1, f32[64,128]{1,0:T(8,128)} %refs_4_.1), custom_call_target="tpu_custom_call" | custom-call | flops 1610612736 | bytes 8388608 | tf_op jit(solution)/shard_map/admm_sweeps/pallas_call | solution.py:267
  110.0 0.6 copy.11
  110.6 0.6 copy.12
  111.2 1.3 %copy.13 = f32[512,1024]{1,0:T(8,128)} copy(f32[512,1024]{1,0:T(8,128)S(1)} %get-tuple-element.5) | data formatting | bytes 4194304

commit v4 on v3

--- a/solution.py
+++ b/solution.py
@@ -21,9 +21,10 @@
 FAR_COL = (9, 8, 7, 6, 10, 5, 11, 4, 12, 3, 13, 2, 14, 1, 15)
 FAR_ROW = (10, 8, 6, 11, 7, 9, 5, 14, 12, 2, 4, 3, 13, 15, 1)
 FAR_PLANE = sorted(
-    ((dy, dx, dc) for dy in range(4) for dx in range(4) for dc in range(2)),
-    key=lambda d: -min(d[0], 4 - d[0]) * 4 - min(d[1], 4 - d[1]) * 4 - d[2],
+    ((dy, dx) for dy in range(4) for dx in range(4)),
+    key=lambda d: -min(d[0], 4 - d[0]) - min(d[1], 4 - d[1]),
 )
+TILES = (2, 1, 3, 0)
 FAR_CHIP = ((2, 1), (1, 1), (3, 1), (2, 0), (0, 1), (1, 0), (3, 0))
 F32 = jnp.float32
 BF16 = jnp.bfloat16
@@ -41,7 +42,7 @@
 
 def kernel(count, obs_hbm, mask_hbm, dual_hbm, u0, v0, u_out, v_out, state,
            obs, mask, ub, vb, gub, gvb, ucat, vcat, chi, clo, pu, pv, sib, ru, rv,
-           nb, load, us, ur, vs, vr, fs, fr, pus, pur, bs, br, pvs, pvr, nss, nsr):
+           pb, nb, pair, load, us, ur, vs, vr, fs, fr, pus, pur, bs, br, pvs, pvr, nss, nsr, cs, cr):
     row = lax.axis_index("row")
     col = lax.axis_index("col")
     z, xlo = col // 2, lax.rem(col, 2)
@@ -49,7 +50,6 @@
     chip = row // 2
     ys = [lax.rem(y + d, 4) for d in range(4)]
     xs = [(lax.rem(xhi * 2 + xlo + d, 4) // 2, lax.rem(xlo + d, 2)) for d in range(4)]
-    cores = (core, 1 - core)
     nr, nc = obs.shape
     ns, ms = nr // N, nc // N
     rank = ub.shape[1]
@@ -125,15 +125,23 @@
         vcat[:, :rank] = vh
         vcat[:, rank:] = vl
 
-        for dm in (2, 1, 3, 0):
+        def tile(dm):
             m = lax.rem(z // 2 + dm, 4)
-            rows = pl.ds(pl.multiple_of(m * TILE, TILE), TILE)
-            a = ucat[rows, :]
+            return m, pl.ds(pl.multiple_of(m * TILE, TILE), TILE)
+
+        def predict(i):
+            a = ucat[tile(TILES[i])[1], :]
             vh = vcat[:, :rank]
             pred = dot(a, jnp.concatenate([vh, vh], axis=1), ((1,), (1,)))
-            pred += dot(a[:, :rank], vcat[:, rank:], ((1,), (1,)))
+            pb[i % 2] = pred + dot(a[:, :rank], vcat[:, rank:], ((1,), (1,)))
+
+        predict(0)
+        for i, dm in enumerate(TILES):
+            if i < 3:
+                predict(i + 1)
+            m, rows = tile(dm)
             old = state[rows, :]
-            wide = obs[rows, :] - pred + old / rho_penalty
+            wide = obs[rows, :] - pb[i % 2] + old / rho_penalty
             c = jnp.clip(wide, LOW, HIGH)
             on = mask[rows, :] == 1
             state[rows, :] = jnp.where(on, rho_penalty * c, old)
@@ -143,10 +151,10 @@
             g = dot(jnp.concatenate([hi, lo], axis=0), vcat[...], ((1,), (0,)))
             g = g[:TILE] + g[TILE:]
             pu[rows, :] = -rho_penalty * (g[:, :rank] + g[:, rank:])
-            for i in range(4):
-                if dm == 0 and i == 0:
+            for j in range(4):
+                if dm == 0 and j == 0:
                     continue
-                to = 4 * m + lax.rem(lax.rem(col, 4) + i, 4)
+                to = 4 * m + lax.rem(lax.rem(col, 4) + j, 4)
                 src = pu.at[pl.ds(pl.multiple_of(to * ns, ns), ns)]
                 send(src, ru.at[col], pus, pur, (row, to))
         ru[col] = pu[own_u, :]
@@ -198,14 +206,18 @@
             gather_v(gvb)
 
         par = lax.rem(t, 2)
-        me = row * N + col
         part = jnp.sum(gu * gu, axis=0, keepdims=True) + jnp.sum(gv * gv, axis=0, keepdims=True)
-        mine = nb.at[par, pl.ds(me, 1)]
-        nb[par, pl.ds(me, 1), :] = part
+        pair[0:1, :] = part
+        send(pair.at[pl.ds(0, 1)], pair.at[pl.ds(8, 1)], cs, cr, sibling)
+
+        wait(pair.at[pl.ds(0, 1)], cr)
+        mine = nb.at[par, pl.ds(chip * N + col, 1)]
+        nb[par, pl.ds(chip * N + col, 1), :] = part + pair[8:9, :]
+
         def tell(zz, skip):
-            for dy, dx, dc in FAR_PLANE[:len(FAR_PLANE) - skip]:
+            for dy, dx in FAR_PLANE[:len(FAR_PLANE) - skip]:
                 send(mine, mine, nss, nsr.at[par],
-                     (ys[dy] * 4 + xs[dx][0] * 2 + cores[dc], zz * 2 + xs[dx][1]))
+                     (ys[dy] * 4 + xs[dx][0] * 2 + core, zz * 2 + xs[dx][1]))
 
         def layer(i, carry):
             dz = 4 + (i + 1) // 2 * (1 - 2 * lax.rem(i, 2))
@@ -219,7 +231,7 @@
         def _():
             forward_v(gvb)
 
-        wait(nb.at[par, pl.ds(0, N * N - 1)], nsr.at[par])
+        wait(nb.at[par, pl.ds(0, N * N // 2 - 1)], nsr.at[par])
         total = jnp.sum(nb[par], axis=(0, 1), keepdims=True)
         step = eta_step / jnp.sqrt(total / count + eps_norm)
 
@@ -238,7 +250,8 @@
         wait(ru.at[pl.ds(0, N - 1)], pus)
         wait(rv.at[pl.ds(0, 7)], pvs)
         wait(sib, bs)
-        wait(nb.at[par, pl.ds(0, N * N - 1)], nss)
+        wait(pair.at[pl.ds(0, 1)], cs)
+        wait(nb.at[par, pl.ds(0, N * N // 2 - 1)], nss)
         return carry
 
     lax.fori_loop(0, ITERS, sweep, 0)
@@ -289,7 +302,9 @@
             pltpu.VMEM((4, 2, ms, rank), F32),
             pltpu.VMEM((N, ns, rank), F32),
             pltpu.VMEM((8, ms, rank), F32),
-            pltpu.VMEM((2, N * N, rank), F32),
+            pltpu.VMEM((2, TILE, nc), F32),
+            pltpu.VMEM((2, N * N // 2, rank), F32),
+            pltpu.VMEM((16, rank), F32),
             pltpu.SemaphoreType.DMA((5,)),
             pltpu.SemaphoreType.DMA,
             pltpu.SemaphoreType.DMA,
@@ -305,6 +320,8 @@
             pltpu.SemaphoreType.DMA,
             pltpu.SemaphoreType.DMA,
             pltpu.SemaphoreType.DMA((2,)),
+            pltpu.SemaphoreType.DMA,
+            pltpu.SemaphoreType.DMA,
         ],
         compiler_params=pltpu.CompilerParams(
             collective_id=0, has_side_effects=True, vmem_limit_bytes=58 * 1024 * 1024
@@ -314,7 +331,15 @@
         ),
         name="admm_sweeps",
     )(observed, mask, dual, row_factor, col_factor)
-    return outs
+    outs = [pltpu.with_memory_space_constraint(o, pltpu.VMEM) for o in outs]
+    return pl.pallas_call(
+        hand_out,
+        out_shape=[jax.ShapeDtypeStruct(o.shape, o.dtype) for o in outs],
+        in_specs=[vmem] * 3,
+        out_specs=[hbm] * 3,
+        scratch_shapes=[pltpu.SemaphoreType.DMA((3,))],
+        name="hand_out",
+    )(*outs)
 
 
 def solution(mesh):

time: 113 us -> 106 us (0.938)
  Pallas kernels: 109 us -> 105 us
  local copies, waits for them, and re-layouts: 2.54 us -> 0 us
    pallas_call x1, Pallas kernels: 109 us -> 104 us  [shards(): pl.pallas_call(body, out_shape=(pltpu.VMEM((ns, rank), F32), pltpu.VMEM((...]
    unnamed x3 -> x0, local copies, waits for them, and re-layouts: 2.54 us -> none
    pallas_call x0 -> x1, Pallas kernels: none -> 1.35 us  [shards(): pl.pallas_call(hand_out, out_shape=[jax.ShapeDtypeStruct(o.shape, o.dtype...]
where the time goes in v4:
time: 106 us
  Pallas kernels  105 us (99%)
    pallas_call x1, Pallas kernels, shards(): pl.pallas_call(body, out_shape=(pltpu.VMEM((ns, rank), F32), pltpu.VMEM((...  104 us

profile of v4, /device:TPU:1, one launch (start us, length us, event | category | flops | bytes accessed | tf_op | source)
XLA Modules:
  0.0 106.1 jit_solution(18183471075760006311)
XLA Ops:
  0.6 104.1 %admm_sweeps.1 = (f32[32,128]{1,0:T(8,128)S(1)}, f32[64,128]{1,0:T(8,128)S(1)}, f32[512,1024]{1,0:T(8,128)S(1)}) custom-call(f32[512,1024]{1,0:T(8,128)} %refs_0_.1, s32[512,1024]{1,0:T(8,128)} %refs_1_.1, f32[512,1024]{1,0:T(8,128)} %refs_2_.1, f32[32,128]{1,0:T(8,128)} %refs_3_.1, f32[64,128]{1,0:T(8,128)} %refs_4_.1), custom_call_target="tpu_custom_call" | custom-call | flops 1610612736 | bytes 8388608 | tf_op jit(solution)/shard_map/admm_sweeps/pallas_call | solution.py:280
  104.7 1.4 %hand_out.1 = (f32[32,128]{1,0:T(8,128)}, f32[64,128]{1,0:T(8,128)}, f32[512,1024]{1,0:T(8,128)}) custom-call(f32[32,128]{1,0:T(8,128)S(1)} %get-tuple-element.6.a0, f32[64,128]{1,0:T(8,128)S(1)} %get-tuple-element.7.a1, f32[512,1024]{1,0:T(8,128)S(1)} %get-tuple-element.8.a2), custom_call_target="tpu_custom_call" | custom-call | tf_op jit(solution)/shard_map/hand_out/pallas_call | solution.py:335

commit v5 on v4

--- a/solution.py
+++ b/solution.py
@@ -42,7 +42,7 @@
 
 def kernel(count, obs_hbm, mask_hbm, dual_hbm, u0, v0, u_out, v_out, state,
            obs, mask, ub, vb, gub, gvb, ucat, vcat, chi, clo, pu, pv, sib, ru, rv,
-           pb, nb, pair, load, us, ur, vs, vr, fs, fr, pus, pur, bs, br, pvs, pvr, nss, nsr, cs, cr):
+           ut, vt, pb, nb, pair, load, us, ur, vs, vr, fs, fr, pus, pur, bs, br, pvs, pvr, nss, nsr, cs, cr):
     row = lax.axis_index("row")
     col = lax.axis_index("col")
     z, xlo = col // 2, lax.rem(col, 2)
@@ -80,9 +80,13 @@
     def chip_at(dy, dx):
         return lax.rem(y + dy, 4) * 2 + (1 - xhi if dx else xhi)
 
-    def gather_u(dst):
+    def part_u(i, h):
+        return pl.ds(pl.multiple_of(i * ns + h * (ns // 2), ns // 2), ns // 2)
+
+    def gather_u(dst, h):
+        own = dst.at[part_u(col, h)]
         for k in FAR_COL:
-            send(dst.at[own_u], dst.at[own_u], us, ur, (row, lax.rem(col + k, N)))
+            send(own, own, us.at[h], ur.at[h], (row, lax.rem(col + k, N)))
 
     def gather_v(dst):
         own = dst.at[chip, core]
@@ -97,9 +101,10 @@
             send(got, got, fs, fr, sibling)
 
     def gathered_u(dst):
-        most = dst.at[pl.ds(0, (N - 1) * ns)]
-        wait(most, ur)
-        wait(most, us)
+        most = dst.at[pl.ds(0, (N - 1) * ns // 2)]
+        for h in range(2):
+            wait(most, ur.at[h])
+            wait(most, us.at[h])
 
     def gathered_v(dst):
         wait(dst.at[:, 0], fr)
@@ -107,7 +112,8 @@
         wait(dst.at[:, 0], fs)
 
     loads[0].wait()
-    gather_u(ub)
+    for h in range(2):
+        gather_u(ub, h)
     loads[1].wait()
     gather_v(vb)
     forward_v(vb)
@@ -121,9 +127,16 @@
         uh, ul = split(ub[...])
         ucat[:, :rank] = uh
         ucat[:, rank:] = ul
+        uth, utl = split(ub[...].T)
+        ut[:rank] = uth
+        ut[rank:] = utl
         vh, vl = split(vb[...].reshape(nc, rank))
         vcat[:, :rank] = vh
         vcat[:, rank:] = vl
+        th, tl = split(vb[...].reshape(nc, rank).T)
+        vt[:rank] = th
+        vt[rank:2 * rank] = th
+        vt[2 * rank:] = tl
 
         def tile(dm):
             m = lax.rem(z // 2 + dm, 4)
@@ -131,9 +144,11 @@
 
         def predict(i):
             a = ucat[tile(TILES[i])[1], :]
-            vh = vcat[:, :rank]
-            pred = dot(a, jnp.concatenate([vh, vh], axis=1), ((1,), (1,)))
-            pb[i % 2] = pred + dot(a[:, :rank], vcat[:, rank:], ((1,), (1,)))
+            pb[i % 2] = dot(jnp.concatenate([a, a[:, :rank]], axis=1), vt[...], ((1,), (0,)))
+
+        def scatter_u(to, h):
+            send(pu.at[part_u(to, h)], ru.at[col, pl.ds(h * (ns // 2), ns // 2)],
+                 pus.at[h], pur.at[h], (row, to))
 
         predict(0)
         for i, dm in enumerate(TILES):
@@ -141,30 +156,30 @@
                 predict(i + 1)
             m, rows = tile(dm)
             old = state[rows, :]
-            wide = obs[rows, :] - pb[i % 2] + old / rho_penalty
+            wide = obs[rows, :] - pb[i % 2] + old
             c = jnp.clip(wide, LOW, HIGH)
             on = mask[rows, :] == 1
-            state[rows, :] = jnp.where(on, rho_penalty * c, old)
+            state[rows, :] = jnp.where(on, c, old)
             hi, lo = split(jnp.where(on, c, 0.0))
             chi[rows, :] = hi
             clo[rows, :] = lo
             g = dot(jnp.concatenate([hi, lo], axis=0), vcat[...], ((1,), (0,)))
             g = g[:TILE] + g[TILE:]
-            pu[rows, :] = -rho_penalty * (g[:, :rank] + g[:, rank:])
+            pu[rows, :] = -(g[:, :rank] + g[:, rank:])
             for j in range(4):
                 if dm == 0 and j == 0:
                     continue
                 to = 4 * m + lax.rem(lax.rem(col, 4) + j, 4)
-                src = pu.at[pl.ds(pl.multiple_of(to * ns, ns), ns)]
-                send(src, ru.at[col], pus, pur, (row, to))
+                scatter_u(to, 0)
+        for k in FAR_COL:
+            scatter_u(lax.rem(col + k, N), 1)
         ru[col] = pu[own_u, :]
 
         def part_v(i, dy):
             yy = lax.rem(y + dy, 4)
             cols = pl.ds(pl.multiple_of(yy * 256, 256), 256)
-            u = ucat[...]
-            g = dot(chi[:, cols], u, ((0,), (0,))) + dot(clo[:, cols], u, ((0,), (0,)))
-            g = -rho_penalty * (g[:, :rank] + g[:, rank:])
+            g = dot(ut[...], chi[:, cols], ((1,), (0,))) + dot(ut[...], clo[:, cols], ((1,), (0,)))
+            g = (-(g[:rank] + g[rank:])).T
             for hi in range(2):
                 for co in range(2):
                     pv[yy, co, hi] = g[(2 * hi + co) * ms:(2 * hi + co + 1) * ms]
@@ -189,13 +204,17 @@
         send_v(3, 0)
         rv[chip] = pv[y, core, xhi]
 
-        wait(ru.at[pl.ds(0, N - 1)], pur)
-        gu = jnp.sum(ru[...], axis=0) + lam_reg * ub[own_u, :]
-        gub[own_u, :] = gu
-
-        @pl.when(jnp.logical_not(last))
-        def _():
-            gather_u(gub)
+        squares = jnp.zeros((1, rank), F32)
+        for h in range(2):
+            rows = slice(h * (ns // 2), (h + 1) * (ns // 2))
+            wait(ru.at[pl.ds(0, N - 1), rows], pur.at[h])
+            gu = jnp.sum(ru[:, rows, :], axis=0) + lam_reg * ub[part_u(col, h), :]
+            gub[part_u(col, h), :] = gu
+            squares += jnp.sum(gu * gu, axis=0, keepdims=True)
+
+            @pl.when(jnp.logical_not(last))
+            def _():
+                gather_u(gub, h)
 
         wait(rv.at[pl.ds(0, 7)], pvr)
         gv = jnp.sum(rv[...], axis=0) + lam_reg * vb[chip, core]
@@ -206,7 +225,7 @@
             gather_v(gvb)
 
         par = lax.rem(t, 2)
-        part = jnp.sum(gu * gu, axis=0, keepdims=True) + jnp.sum(gv * gv, axis=0, keepdims=True)
+        part = squares + jnp.sum(gv * gv, axis=0, keepdims=True)
         pair[0:1, :] = part
         send(pair.at[pl.ds(0, 1)], pair.at[pl.ds(8, 1)], cs, cr, sibling)
 
@@ -247,7 +266,8 @@
             u_out[...] = ub[own_u, :] - step * gub[own_u, :]
             v_out[...] = vb[chip, core] - step * gvb[chip, core]
 
-        wait(ru.at[pl.ds(0, N - 1)], pus)
+        for h in range(2):
+            wait(ru.at[pl.ds(0, N - 1), pl.ds(0, ns // 2)], pus.at[h])
         wait(rv.at[pl.ds(0, 7)], pvs)
         wait(sib, bs)
         wait(pair.at[pl.ds(0, 1)], cs)
@@ -302,18 +322,20 @@
             pltpu.VMEM((4, 2, ms, rank), F32),
             pltpu.VMEM((N, ns, rank), F32),
             pltpu.VMEM((8, ms, rank), F32),
+            pltpu.VMEM((2 * rank, nr), BF16),
+            pltpu.VMEM((3 * rank, nc), BF16),
             pltpu.VMEM((2, TILE, nc), F32),
             pltpu.VMEM((2, N * N // 2, rank), F32),
             pltpu.VMEM((16, rank), F32),
             pltpu.SemaphoreType.DMA((5,)),
-            pltpu.SemaphoreType.DMA,
-            pltpu.SemaphoreType.DMA,
+            pltpu.SemaphoreType.DMA((2,)),
+            pltpu.SemaphoreType.DMA((2,)),
             pltpu.SemaphoreType.DMA,
             pltpu.SemaphoreType.DMA((7,)),
             pltpu.SemaphoreType.DMA,
             pltpu.SemaphoreType.DMA,
-            pltpu.SemaphoreType.DMA,
-            pltpu.SemaphoreType.DMA,
+            pltpu.SemaphoreType.DMA((2,)),
+            pltpu.SemaphoreType.DMA((2,)),
             pltpu.SemaphoreType.DMA,
             pltpu.SemaphoreType.DMA((4,)),
             pltpu.SemaphoreType.DMA,

time: 106 us -> 103 us (0.972)
  Pallas kernels: 105 us -> 103 us
    pallas_call x1, Pallas kernels: 104 us -> 101 us  [shards(): pl.pallas_call(body, out_shape=(pltpu.VMEM((ns, rank), F32), pltpu.VMEM((...]
where the time goes in v5:
time: 103 us
  Pallas kernels  103 us (100%)
    pallas_call x1, Pallas kernels, shards(): pl.pallas_call(body, out_shape=(pltpu.VMEM((ns, rank), F32), pltpu.VMEM((...  101 us

profile of v5, /device:TPU:1, one launch (start us, length us, event | category | flops | bytes accessed | tf_op | source)
XLA Modules:
  0.0 103.2 jit_solution(12995094273586551931)
XLA Ops:
  0.6 101.2 %admm_sweeps.1 = (f32[32,128]{1,0:T(8,128)S(1)}, f32[64,128]{1,0:T(8,128)S(1)}, f32[512,1024]{1,0:T(8,128)S(1)}) custom-call(f32[512,1024]{1,0:T(8,128)} %refs_0_.1, s32[512,1024]{1,0:T(8,128)} %refs_1_.1, f32[512,1024]{1,0:T(8,128)} %refs_2_.1, f32[32,128]{1,0:T(8,128)} %refs_3_.1, f32[64,128]{1,0:T(8,128)} %refs_4_.1), custom_call_target="tpu_custom_call" | custom-call | flops 1610612736 | bytes 8388608 | tf_op jit(solution)/shard_map/admm_sweeps/pallas_call | solution.py:300
  101.9 1.4 %hand_out.1 = (f32[32,128]{1,0:T(8,128)}, f32[64,128]{1,0:T(8,128)}, f32[512,1024]{1,0:T(8,128)}) custom-call(f32[32,128]{1,0:T(8,128)S(1)} %get-tuple-element.6.a0, f32[64,128]{1,0:T(8,128)S(1)} %get-tuple-element.7.a1, f32[512,1024]{1,0:T(8,128)S(1)} %get-tuple-element.8.a2), custom_call_target="tpu_custom_call" | custom-call | tf_op jit(solution)/shard_map/hand_out/pallas_call | solution.py:357

commit v6 on v5

--- a/solution.py
+++ b/solution.py
@@ -112,10 +112,10 @@
         wait(dst.at[:, 0], fs)
 
     loads[0].wait()
+    loads[1].wait()
+    gather_v(vb)
     for h in range(2):
         gather_u(ub, h)
-    loads[1].wait()
-    gather_v(vb)
     forward_v(vb)
     for c in loads[2:]:
         c.wait()
@@ -278,8 +278,10 @@
 
 
 def hand_out(a0, a1, a2, b0, b1, b2, sem):
+    rows = a2.shape[0] // 4
+    parts = [(a2.at[pl.ds(i * rows, rows)], b2.at[pl.ds(i * rows, rows)]) for i in range(4)]
     copies = [pltpu.make_async_copy(a, b, sem.at[i])
-              for i, (a, b) in enumerate(((a2, b2), (a0, b0), (a1, b1)))]
+              for i, (a, b) in enumerate(parts + [(a0, b0), (a1, b1)])]
     for c in copies:
         c.start()
     for c in copies:
@@ -359,7 +361,7 @@
         out_shape=[jax.ShapeDtypeStruct(o.shape, o.dtype) for o in outs],
         in_specs=[vmem] * 3,
         out_specs=[hbm] * 3,
-        scratch_shapes=[pltpu.SemaphoreType.DMA((3,))],
+        scratch_shapes=[pltpu.SemaphoreType.DMA((6,))],
         name="hand_out",
     )(*outs)
 

time: 103 us -> 103 us (level)
  no operation moved by 1% of the time
where the time goes in v6:
time: 103 us
  Pallas kernels  102 us (99%)
    pallas_call x1, Pallas kernels, shards(): pl.pallas_call(body, out_shape=(pltpu.VMEM((ns, rank), F32), pltpu.VMEM((...  101 us

profile of v6, /device:TPU:1, one launch (start us, length us, event | category | flops | bytes accessed | tf_op | source)
XLA Modules:
  0.0 103.1 jit_solution(9506440371731910903)
XLA Ops:
  0.6 101.1 %admm_sweeps.1 = (f32[32,128]{1,0:T(8,128)S(1)}, f32[64,128]{1,0:T(8,128)S(1)}, f32[512,1024]{1,0:T(8,128)S(1)}) custom-call(f32[512,1024]{1,0:T(8,128)} %refs_0_.1, s32[512,1024]{1,0:T(8,128)} %refs_1_.1, f32[512,1024]{1,0:T(8,128)} %refs_2_.1, f32[32,128]{1,0:T(8,128)} %refs_3_.1, f32[64,128]{1,0:T(8,128)} %refs_4_.1), custom_call_target="tpu_custom_call" | custom-call | flops 1610612736 | bytes 8388608 | tf_op jit(solution)/shard_map/admm_sweeps/pallas_call | solution.py:302
  101.7 1.4 %hand_out.1 = (f32[32,128]{1,0:T(8,128)}, f32[64,128]{1,0:T(8,128)}, f32[512,1024]{1,0:T(8,128)}) custom-call(f32[32,128]{1,0:T(8,128)S(1)} %get-tuple-element.6.a0, f32[64,128]{1,0:T(8,128)S(1)} %get-tuple-element.7.a1, f32[512,1024]{1,0:T(8,128)S(1)} %get-tuple-element.8.a2), custom_call_target="tpu_custom_call" | custom-call | tf_op jit(solution)/shard_map/hand_out/pallas_call | solution.py:359
